TPU v7x, 32 devices: a whole 2x2x4 slice. The times are simulated.
32 devices in a mesh: ctx: 8 (over z, x), head: 4 (over y, core).
Axes of the slice: x: 2, y: 2, z: 4, core: 2. Of those that a mesh axis runs over, the one named last changes fastest.
Arguments:
- query_rows: bfloat16 [24576, 4096], P('ctx', 'head'), may hold values from -6 to 6
- key_rows: bfloat16 [24576, 4096], P('ctx', 'head'), may hold values from -6 to 6
- value_rows: bfloat16 [24576, 4096], P('ctx', 'head'), may hold values from -220 to 220
- out_gain: bfloat16 [4096], P('head'), may hold values from 0.5 to 1.5
- doc_starts: int32 [16], replicated, may hold values from 0 to 24575, as said below
Outputs:
- normed: bfloat16 [24576, 4096], P('ctx', 'head')
Inputs may be any that keep to these rules, and one draw needn't show every extreme that they name: `doc_starts`: ascending and distinct, the first entry 0, the last entry 24575.
All inputs are finite; a program needn't handle non-finite values.
Results may differ from a plain program's by a relative error of at most 0.001.
Values sent between devices are 32-bit elements; how exact they have to be, the bound alone decides.
No kernel may reach another device: no remote copies, remote signals or barrier semaphores. Data moves between devices by JAX's collectives and lax.ppermute only.
A program may use at most 192 MiB of HBM per device.

v0:
```python
import functools
import jax
import jax.numpy as jnp
from jax import lax
from jax.experimental import pallas as pl
from jax.experimental.pallas import tpu as pltpu
from jax.sharding import PartitionSpec as P

HEADS = 32
HD = 128
CH = 128
STEP = 512
GROUPS = 2
AHEAD = 4
bf16, f32, i32 = jnp.bfloat16, jnp.float32, jnp.int32
VM = pl.BlockSpec(memory_space=pltpu.VMEM)
SM = pl.BlockSpec(memory_space=pltpu.SMEM)
HB = pl.BlockSpec(memory_space=pltpu.HBM)


def params(mib):
    return pltpu.CompilerParams(vmem_limit_bytes=mib << 20)


def mm(a, b):
    return jnp.dot(a, b, preferred_element_type=f32)


def split(x):
    hi = x.astype(bf16)
    return hi, (x - hi.astype(f32)).astype(bf16)


def diagonal(a, b):
    zero = jnp.zeros((HD, HD), a.dtype)
    return jnp.concatenate([jnp.concatenate([a, zero], 1), jnp.concatenate([zero, b], 1)], 0)


def starts_in(starts_ref, low, high):
    count = jnp.int32(0)
    for d in range(starts_ref.shape[0]):
        count += ((starts_ref[d] >= low) & (starts_ref[d] < high)).astype(i32)
    return count


def states_kernel(col, first, pairs, starts_ref, dev_ref, k_hbm, v_hbm, q_hbm, kt_ref, v_ref, q_ref, st_ref, sum_ref, *rest):
    if first:
        mask_ref, live_ref, hops_ref, kbuf, sem = rest
    else:
        kbuf, sem = rest
    tokens, feats = v_ref.shape
    heads, chunks, steps, per = feats // HD, tokens // CH, tokens // STEP, STEP // CH
    copies = []
    for n, (src, dst) in enumerate(((k_hbm, kbuf), (v_hbm, v_ref), (q_hbm, q_ref))):
        copies.append([])
        for p in range(steps):
            rows = pl.ds(p * STEP, STEP)
            copies[n].append(pltpu.make_async_copy(src.at[rows, pl.ds(col, feats)], dst.at[rows], sem.at[n, p]))
    for p in range(steps):
        copies[0][p].start()
        copies[1][p].start()
    for p in range(steps):
        copies[2][p].start()
    if first:
        hops, streak, through = jnp.int32(0), jnp.int32(0), jnp.int32(1)
        for p in range(pairs):
            bare = starts_in(starts_ref, p * 2 * tokens, (p + 1) * 2 * tokens) == 0
            through = jnp.where((dev_ref[0] // 2 == p + 1) & ~bare, 0, through)
            if 0 < p < pairs - 1:
                streak = jnp.where(bare, streak + 1, 0)
                hops = jnp.maximum(hops, streak)
        hops_ref[0] = hops
        hops_ref[1] = through
    base = lax.broadcasted_iota(i32, (chunks, CH), 0) * CH
    at = base + lax.broadcasted_iota(i32, (chunks, CH), 1)
    start = jnp.full((chunks, CH), -1, i32)
    for d in range(starts_ref.shape[0]):
        s = starts_ref[d] - dev_ref[0] * tokens
        start = jnp.where(at >= s, jnp.maximum(start, s), start)
    last = start[:, CH - 1:]
    tail = (at >= last).astype(f32)
    keep = (last < base).astype(f32)
    if first:
        rel = (start - base).astype(f32)
        row = lax.broadcasted_iota(i32, (CH, CH), 0).astype(f32)
        lane = lax.broadcasted_iota(i32, (CH, CH), 1).astype(f32)
        causal = (lane <= row).astype(f32)
        for c in range(chunks):
            lower = jnp.broadcast_to(rel[c:c + 1], (CH, CH)).T
            mask_ref[c * CH:(c + 1) * CH, :] = jnp.where(lane >= lower, causal, 0.0)
            live_ref[c * CH:(c + 1) * CH, :] = (lower < 0.0).astype(f32).astype(bf16)
    for h in range(heads):
        st_ref[0, h] = jnp.zeros((HD, HD), f32)

    def advance(c, h, added):
        for i in (h, h + 1):
            s = st_ref[c, i] * keep[c:c + 1] + added[:, (i - h) * HD:(i - h + 1) * HD]
            if c + 1 < chunks:
                st_ref[c + 1, i] = s
            else:
                sum_ref[i] = s

    waiting = []
    for c in range(chunks):
        if c % per == 0:
            copies[0][c // per].wait()
            copies[1][c // per].wait()
        rows = slice(c * CH, (c + 1) * CH)
        t = tail[c:c + 1].astype(bf16)
        for h in range(0, heads, 2):
            a, b = slice(h * HD, (h + 1) * HD), slice((h + 1) * HD, (h + 2) * HD)
            ka, kb = kbuf[rows, a].T, kbuf[rows, b].T
            kt_ref[a, rows] = ka
            kt_ref[b, rows] = kb
            pair = jnp.concatenate([ka * t, kb * t], 1)
            waiting.append((c, h, mm(pair, diagonal(v_ref[rows, a], v_ref[rows, b]))))
            if len(waiting) > AHEAD:
                advance(*waiting.pop(0))
    for item in waiting:
        advance(*item)
    for p in range(steps):
        copies[2][p].wait()


def states_call(col, feats, first, pairs, starts, dev, k, v, q):
    tokens = k.shape[0]
    heads, chunks, steps = feats // HD, tokens // CH, tokens // STEP
    rows = pltpu.VMEM((tokens, feats), bf16)
    out = [pltpu.VMEM((feats, tokens), bf16), rows, rows,
           pltpu.VMEM((chunks, heads, HD, HD), f32), pltpu.VMEM((heads, HD, HD), f32)]
    if first:
        out += [pltpu.VMEM((tokens, CH), f32), pltpu.VMEM((tokens, CH), bf16), jax.ShapeDtypeStruct((2,), i32)]
    k, v, q = (pltpu.with_memory_space_constraint(x, pltpu.HBM) for x in (k, v, q))
    return pl.pallas_call(
        functools.partial(states_kernel, col, first, pairs), in_specs=[SM, SM, HB, HB, HB],
        out_specs=[VM] * 7 + [SM] if first else [VM] * 5, out_shape=out,
        scratch_shapes=[pltpu.VMEM((tokens, feats), bf16),
                        pltpu.SemaphoreType.DMA((3, steps))],
        compiler_params=params(8), name="states")(starts, dev, k, v, q)


def within_kernel(mask_ref, q_ref, kt_ref, v_ref, o_ref):
    tokens, feats = v_ref.shape

    def finish(rows, both, a, b, hi, lo):
        vd = diagonal(v_ref[rows, a], v_ref[rows, b])
        o_ref[rows, both] = mm(hi, vd) + mm(lo, vd)

    waiting = []
    for c in range(tokens // CH):
        rows = slice(c * CH, (c + 1) * CH)
        m = mask_ref[rows, :]
        m = jnp.concatenate([m, m], 1)
        for h in range(0, feats, 2 * HD):
            both, a, b = slice(h, h + 2 * HD), slice(h, h + HD), slice(h + HD, h + 2 * HD)
            scores = mm(q_ref[rows, both], diagonal(kt_ref[a, rows], kt_ref[b, rows]))
            waiting.append((rows, both, a, b) + split(scores * m))
            if len(waiting) > AHEAD:
                finish(*waiting.pop(0))
    for item in waiting:
        finish(*item)


def within_call(mask, q, kt, v):
    return pl.pallas_call(
        within_kernel, in_specs=[VM] * 4, out_specs=VM, out_shape=pltpu.VMEM(v.shape, f32),
        compiler_params=params(8), name="within")(mask, q, kt, v)


def joined_kernel(starts_ref, dev_ref, own_ref, other_ref, o_ref):
    tokens = dev_ref[1]
    odd = dev_ref[0] % 2
    low = (dev_ref[0] - odd + 1) * tokens
    empty = (starts_in(starts_ref, low, low + tokens) == 0).astype(f32)
    one = jnp.float32(1.0)
    o_ref[...] = own_ref[...] * jnp.where(odd == 1, one, empty) + other_ref[...] * jnp.where(odd == 1, empty, one)


def joined_call(starts, dev, own, other):
    return pl.pallas_call(
        joined_kernel, in_specs=[SM, SM, VM, VM], out_specs=VM, out_shape=pltpu.VMEM(own.shape, f32),
        compiler_params=params(8), name="joined")(starts, dev, own, other)


def across_kernel(last, starts_ref, dev_ref, live_ref, q_ref, st_ref, other_ref, planes_ref, att_ref, *rest):
    if last:
        sq_in, o_ref, sq_ref, ent = rest
    else:
        o_ref, sq_ref, ent = rest
    tokens, feats = q_ref.shape
    heads = feats // HD
    dev = dev_ref[0]
    odd = dev % 2
    anchor = dev * tokens
    empty = (starts_in(starts_ref, anchor - tokens, anchor) == 0).astype(f32)
    one, zero = jnp.float32(1.0), jnp.float32(0.0)
    ent[...] = other_ref[...] * jnp.where(odd == 1, one, zero) + planes_ref[...] * jnp.where(
        dev < 2, zero, jnp.where(odd == 1, empty, one))
    first = jnp.int32(tokens)
    for d in range(starts_ref.shape[0]):
        s = starts_ref[d] - anchor
        first = jnp.where(s >= 0, jnp.minimum(first, s), first)

    totals = [None] * (tokens // CH)

    def finish(c, h, x):
        rows, cols = slice(c * CH, (c + 1) * CH), slice(h * HD, (h + 2) * HD)
        o = att_ref[rows, cols] + x
        o_ref[rows, cols] = o
        o = o * o
        o = o[:, :HD] + o[:, HD:]
        totals[c] = o if h == 0 else totals[c] + o
        if h == heads - 2:
            line = jnp.sum(totals[c].T, axis=0, keepdims=True)
            sq_ref[c:c + 1, :] = line + sq_in[c:c + 1, :] if last else line

    waiting = []
    for c in range(tokens // CH):
        rows = slice(c * CH, (c + 1) * CH)
        lv = live_ref[rows, :]
        reach = jnp.where(c * CH <= first, one, zero)
        for h in range(0, heads, 2):
            x = []
            for i in (h, h + 1):
                parts = split(st_ref[c, i] + ent[i] * reach)
                y = mm(q_ref[rows, i * HD:(i + 1) * HD] * lv, jnp.concatenate(parts, 1))
                x.append(y[:, :HD] + y[:, HD:])
            waiting.append((c, h, jnp.concatenate(x, 1)))
            if len(waiting) > AHEAD:
                finish(*waiting.pop(0))
    for item in waiting:
        finish(*item)


def across_call(starts, dev, live, q, st, other, planes, att, sq=None):
    tokens, feats = att.shape
    last = sq is not None
    args = (starts, dev, live, q, st, other, planes, att) + ((sq,) if last else ())
    return pl.pallas_call(
        functools.partial(across_kernel, last), in_specs=[SM, SM] + [VM] * (len(args) - 2), out_specs=[VM, VM],
        out_shape=[pltpu.VMEM(att.shape, f32), pltpu.VMEM((tokens // CH, CH), f32)],
        scratch_shapes=[pltpu.VMEM(other.shape, f32)],
        input_output_aliases={7: 0}, compiler_params=params(8), name="across")(*args)


def norm_kernel(width, groups, *refs):
    atts, (mine_ref, theirs_ref, gain_ref, o_hbm, buf, sem) = refs[:groups], refs[groups:]
    tokens, feats = atts[0].shape
    steps, per = tokens // STEP, STEP // CH
    scale = lax.rsqrt((mine_ref[...] + theirs_ref[...]) / width + 1e-6)
    gain = gain_ref[...].astype(f32)
    copies = []
    for p in range(steps):
        for c in range(p * per, (p + 1) * per):
            rows = slice(c * CH, (c + 1) * CH)
            r = jnp.broadcast_to(scale[c:c + 1], (CH, CH)).T
            for g in range(groups):
                for h in range(feats // HD):
                    cols, place = slice(h * HD, (h + 1) * HD), slice(g * feats + h * HD, g * feats + (h + 1) * HD)
                    buf[rows, place] = (atts[g][rows, cols] * r * gain[:, place]).astype(bf16)
        rows = pl.ds(p * STEP, STEP)
        copy = pltpu.make_async_copy(buf.at[rows], o_hbm.at[rows], sem.at[p])
        copy.start()
        copies.append(copy)
    for copy in copies:
        copy.wait()


def norm_call(width, atts, mine, theirs, gain):
    tokens, feats = atts[0].shape
    groups = len(atts)
    atts = [pltpu.with_memory_space_constraint(x, pltpu.VMEM) for x in atts]
    return pl.pallas_call(
        functools.partial(norm_kernel, width, groups), in_specs=[VM] * (groups + 3), out_specs=HB,
        out_shape=pltpu.HBM((tokens, feats * groups), bf16),
        scratch_shapes=[pltpu.VMEM((tokens, feats * groups), bf16), pltpu.SemaphoreType.DMA((tokens // STEP,))],
        compiler_params=params(10), name="norm")(*atts, mine, theirs, gain)


def core(general, dev, query_rows, key_rows, value_rows, out_gain, doc_starts):
    features = query_rows.shape[1]
    slabs, ways = lax.axis_size("ctx"), lax.axis_size("head")
    feats = features // GROUPS
    beside = [(i, i ^ 1) for i in range(slabs)]
    onward = [(i, i + 2) for i in range(slabs - 2)]
    states, other = [], []
    for g in range(GROUPS):
        states.append(states_call(g * feats, feats, g == 0, slabs // 2, doc_starts, dev, key_rows, value_rows, query_rows))
        other.append(lax.ppermute(states[g][4], "ctx", beside))
    mask, live, hops = states[0][5:]
    planes, atts = [], []
    for g in range(GROUPS):
        kt, v, q = states[g][:3]
        atts.append(within_call(mask, q, kt, v))
        if g == 0:
            other[g], atts[g] = lax.optimization_barrier((other[g], atts[g]))
        planes.append(lax.ppermute(joined_call(doc_starts, dev, states[g][4], other[g]), "ctx", onward))
    sq = None
    for g in range(GROUPS):
        q, st = states[g][2:4]
        far = planes[g]
        if general:
            through = hops[1].astype(f32)
            far = lax.fori_loop(0, hops[0], lambda _, p: planes[g] + through * lax.ppermute(p, "ctx", onward), far)
        atts[g], sq = across_call(doc_starts, dev, live, q, st, other[g], far, atts[g], sq)
    mine = sq
    for bit in range(ways.bit_length() - 1):
        theirs = lax.ppermute(mine, "head", [(i, i ^ (1 << bit)) for i in range(ways)])
        if bit < ways.bit_length() - 2:
            mine = mine + theirs
    return norm_call(HEADS * HD, atts, mine, theirs, out_gain.reshape(1, -1)), hops


def shards(query_rows, key_rows, value_rows, out_gain, doc_starts):
    tokens = query_rows.shape[0]
    dev = jnp.stack([lax.axis_index("ctx").astype(i32), jnp.int32(tokens)])
    args = (dev, query_rows, key_rows, value_rows, out_gain, doc_starts)
    near, hops = core(False, *args)
    return lax.cond(hops[0] > 0, lambda near, *args: core(True, *args)[0], lambda near, *args: near, near, *args)


def solution(mesh):
    placed = (P("ctx", "head"), P("ctx", "head"), P("ctx", "head"), P("head"), P())
    return jax.shard_map(
        shards, mesh=mesh, in_specs=placed, out_specs=P("ctx", "head"), check_vma=False
    )
```

profile of v0, /device:TPU:0, one launch (start us, length us, event | category | flops | bytes accessed | tf_op | source)
XLA Modules:
  0.0 43.9 jit_solution(17563977872346021135)
XLA Ops:
  0.0 0.1 pad_add_fusion.dev_ref
  0.1 0.0 copy-start.25
  0.1 5.3 %states.6 = (bf16[512,3072]{1,0:T(8,128)(2,1)S(1)}, bf16[3072,512]{1,0:T(8,128)(2,1)S(1)}, bf16[3072,512]{1,0:T(8,128)(2,1)S(1)}, f32[24,4,128,128]{3,2,1,0:T(8,...) custom-call(s32[16]{0:T(128)} %starts_ref.11, ...), custom_call_target="tpu_custom_call" | custom-call | tf_op jit(solution)/shard_map/states/pallas_call | solution.py:134
  5.4 3.0 %collective-permute-start.8 = (f32[4,128,128]{2,1,0:T(8,128)S(1)}, f32[4,128,128]{2,1,0:T(8,128)S(1)}, u32[]{:S(2)}, u32[]{:S(2)}) collective-permute-start(f32[4,128,128]{2,1,0:T(8,128)S(1)} %get-tuple-element.125.own_ref), channel_id=1, source_target_pairs={{0,4},{4,0},{8,12},{12,8},{16,20},{20,16},{24,28},{28,24},{1,5},{5... | collective-permute-start | bytes 786440 | tf_op jit(solution)/shard_map/ppermute | solution.py:289
  8.4 0.0 copy-done.25
  8.4 4.4 %states.7 = (bf16[512,3072]{1,0:T(8,128)(2,1)S(1)}, bf16[3072,512]{1,0:T(8,128)(2,1)S(1)}, bf16[3072,512]{1,0:T(8,128)(2,1)S(1)}, f32[24,4,128,128]{3,2,1,0:T(8,128)S(1)}, f32[4,128,128]{2,1,0:T(8,128)S(1)}) custom-call(s32[16]{0:T(128)S(1)} %copy-done.25, s32[2]{0:T(128)S(1)} %pad_add_fusion.dev_ref, bf16[3072,1024]{1,0:T(8,128)(2,1)} %k_hbm.3, ...), custom_call_target="tpu_custom_call" | custom-call | tf_op jit(solution)/shard_map/states/pallas_call | solution.py:134
  12.8 0.1 collective-permute-start.10
  12.9 2.8 %within.6.att_ref = f32[3072,512]{1,0:T(8,128)S(1)} custom-call(f32[3072,128]{1,0:T(8,128)S(1)} %get-tuple-element.126.mask_ref, bf16[3072,512]{1,0:T(8,128)(2,1)S(1)} %get-tuple-element.123.q_ref, bf16[512,3072]{1,0:T(8,128)(2,1)S(1)} %get-tuple-element.127.kt_ref, bf16[3072,512]{1,0:T(8,128)(2,1)S(1)} %get-tuple-element.128.v_ref), custom_call_target="tpu_custom_call" | custom-call | tf_op jit(solution)/shard_map/within/pallas_call | solution.py:165
  15.7 0.0 collective-permute-done.8.other_ref
  15.7 0.6 %joined.6 = f32[4,128,128]{2,1,0:T(8,128)S(1)} custom-call(s32[16]{0:T(128)S(1)} %copy-done.25, s32[2]{0:T(128)S(1)} %pad_add_fusion.dev_ref, f32[4,128,128]{2,1,0:T(8,128)S(1)} %get-tuple-element.125.own_ref, f32[4,128,128]{2,1,0:T(8,128)S(1)} %collective-permute-done.8.other_ref), custom_call_target="tpu_custom_call" | custom-call | tf_op jit(solution)/shard_map/joined/pallas_call | solution.py:180
  16.4 4.0 %collective-permute-start.9 = (f32[4,128,128]{2,1,0:T(8,128)S(1)}, f32[4,128,128]{2,1,0:T(8,128)S(1)}, u32[]{:S(2)}, u32[]{:S(2)}) collective-permute-start(f32[4,128,128]{2,1,0:T(8,128)S(1)} %joined.6), channel_id=1, source_target_pairs={{0,8},{4,12},{8,16},{12,20},{16,24},{20,28},{1,9},{5,13},{9,17},{1... | collective-permute-start | bytes 786440 | tf_op jit(solution)/shard_map/ppermute | solution.py:297
  20.4 0.3 collective-permute-done.10.other_ref
  20.7 0.6 %joined.7 = f32[4,128,128]{2,1,0:T(8,128)S(1)} custom-call(s32[16]{0:T(128)S(1)} %copy-done.25, s32[2]{0:T(128)S(1)} %pad_add_fusion.dev_ref, f32[4,128,128]{2,1,0:T(8,128)S(1)} %get-tuple-element.134.own_ref, f32[4,128,128]{2,1,0:T(8,128)S(1)} %collective-permute-done.10.other_ref), custom_call_target="tpu_custom_call" | custom-call | tf_op jit(solution)/shard_map/joined/pallas_call | solution.py:180
  21.3 3.7 %collective-permute-start.11 = (f32[4,128,128]{2,1,0:T(8,128)S(1)}, f32[4,128,128]{2,1,0:T(8,128)S(1)}, u32[]{:S(2)}, u32[]{:S(2)}) collective-permute-start(f32[4,128,128]{2,1,0:T(8,128)S(1)} %joined.7), channel_id=1, source_target_pairs={{0,8},{4,12},{8,16},{12,20},{16,24},{20,28},{1,9},{5,13},{9,17},{1... | collective-permute-start | bytes 786440 | tf_op jit(solution)/shard_map/ppermute | solution.py:297
  25.0 2.8 %within.7.att_ref = f32[3072,512]{1,0:T(8,128)S(1)} custom-call(f32[3072,128]{1,0:T(8,128)S(1)} %get-tuple-element.126.mask_ref, bf16[3072,512]{1,0:T(8,128)(2,1)S(1)} %get-tuple-element.132.q_ref, bf16[512,3072]{1,0:T(8,128)(2,1)S(1)} %get-tuple-element.135.kt_ref, bf16[3072,512]{1,0:T(8,128)(2,1)S(1)} %get-tuple-element.136.v_ref), custom_call_target="tpu_custom_call" | custom-call | tf_op jit(solution)/shard_map/within/pallas_call | solution.py:165
  27.8 0.0 collective-permute-done.9.planes_ref
  27.8 3.8 %across.6 = (f32[3072,512]{1,0:T(8,128)S(1)}, f32[24,128]{1,0:T(8,128)S(1)}) custom-call(s32[16]{0:T(128)S(1)} %copy-done.25, s32[2]{0:T(128)S(1)} %pad_add_fusion.dev_ref, bf16[3072,128]{1,0:T(8,128)(2,1)S(1)} %get-tuple-element.122.live_ref, bf16[3072,512]{1,0:T(8,128)(2,1)S(1)} %get-tuple-element.123.q_ref, ...), custom_call_target="tpu_custom_call", output_to_operand_aliasing={{0}: (7, {})} | custom-call | tf_op jit(solution)/shard_map/across/pallas_call | solution.py:239
  31.6 0.0 collective-permute-done.11.planes_ref
  31.6 0.0 copy-start.26
  31.6 3.8 %across.7 = (f32[3072,512]{1,0:T(8,128)S(1)}, f32[24,128]{1,0:T(8,128)S(1)}) custom-call(s32[16]{0:T(128)S(1)} %copy-done.25, s32[2]{0:T(128)S(1)} %pad_add_fusion.dev_ref, bf16[3072,128]{1,0:T(8,128)(2,1)S(1)} %get-tuple-element.122.live_ref, bf16[3072,512]{1,0:T(8,128)(2,1)S(1)} %get-tuple-element.132.q_ref, ...), custom_call_target="tpu_custom_call", output_to_operand_aliasing={{0}: (7, {})} | custom-call | tf_op jit(solution)/shard_map/across/pallas_call | solution.py:239
  35.4 0.1 collective-permute-start.12
  35.5 1.2 %collective-permute-done.12 = f32[24,128]{1,0:T(8,128)S(1)} collective-permute-done((f32[24,128]{1,0:T(8,128)S(1)}, f32[24,128]{1,0:T(8,128)S(1)}, u32[]{:S(2)}, u32[]{:S(2)}) %collective-permute-start.12) | collective-permute-done | bytes 12320 | tf_op jit(solution)/shard_map/ppermute | solution.py:308
  36.7 1.5 %collective-permute-start.13 = (f32[24,128]{1,0:T(8,128)S(1)}, f32[24,128]{1,0:T(8,128)S(1)}, u32[]{:S(2)}, u32[]{:S(2)}) collective-permute-start(f32[24,128]{1,0:T(8,128)S(1)} %add.18.refs_2_), channel_id=1, source_target_pairs={{0,2},{1,3},{2,0},{3,1},{4,6},{5,7},{6,4},{7,5},{8,10},{9,11},{10,... | collective-permute-start | bytes 36872 | tf_op jit(solution)/shard_map/ppermute | solution.py:308
  38.2 0.0 copy-done.26
  38.3 2.1 %collective-permute-done.13.refs_3_ = f32[24,128]{1,0:T(8,128)S(1)} collective-permute-done((f32[24,128]{1,0:T(8,128)S(1)}, f32[24,128]{1,0:T(8,128)S(1)}, u32[]{:S(2)}, u32[]{:S(2)}) %collective-permute-start.13) | collective-permute-done | bytes 12320 | tf_op jit(solution)/shard_map/ppermute | solution.py:308
  40.4 3.0 %norm.3 = bf16[3072,1024]{1,0:T(8,128)(2,1)} custom-call(f32[3072,512]{1,0:T(8,128)S(1)} %get-tuple-element.131.refs_0_, f32[3072,512]{1,0:T(8,128)S(1)} %get-tuple-element.138.refs_1_, f32[24,128]{1,0:T(8,128)S(1)} %add.18.refs_2_, f32[24,128]{1,0:T(8,128)S(1)} %collective-permute-done.13.refs_3_, bf16[1,1024]{1,0:T(2,128)(2,1)S(1)} %reshape.11.refs_4_), custom_call_target="tpu_custom_call" | custom-call | tf_op jit(solution)/shard_map/norm/pallas_call | solution.py:273
  43.4 0.3 conditional.1
  (2 shorter events, 0.0 us)
Async XLA Ops:
  0.1 8.4 %copy-start.25 = (s32[16]{0:T(128)S(1)}, s32[16]{0:T(128)}, u32[]{:S(2)}) copy-start(s32[16]{0:T(128)} %starts_ref.11) | copy-start | bytes 196
  5.4 10.3 %collective-permute-start.8 = (f32[4,128,128]{2,1,0:T(8,128)S(1)}, f32[4,128,128]{2,1,0:T(8,128)S(1)}, u32[]{:S(2)}, u32[]{:S(2)}) collective-permute-start(f32[4,128,128]{2,1,0:T(8,128)S(1)} %get-tuple-element.125.own_ref), channel_id=1, source_target_pairs={{0,4},{4,0},{8,12},{12,8},{16,20},{20,16},{24,28},{28,24},{1,5},{5... | collective-permute-start | bytes 786440 | tf_op jit(solution)/shard_map/ppermute | solution.py:289
  12.8 7.8 %collective-permute-start.10 = (f32[4,128,128]{2,1,0:T(8,128)S(1)}, f32[4,128,128]{2,1,0:T(8,128)S(1)}, u32[]{:S(2)}, u32[]{:S(2)}) collective-permute-start(f32[4,128,128]{2,1,0:T(8,128)S(1)} %get-tuple-element.134.own_ref), channel_id=1, source_target_pairs={{0,4},{4,0},{8,12},{12,8},{16,20},{20,16},{24,28},{28,24},{1,5},{5... | collective-permute-start | bytes 786440 | tf_op jit(solution)/shard_map/ppermute | solution.py:289
  16.4 11.4 %collective-permute-start.9 = (f32[4,128,128]{2,1,0:T(8,128)S(1)}, f32[4,128,128]{2,1,0:T(8,128)S(1)}, u32[]{:S(2)}, u32[]{:S(2)}) collective-permute-start(f32[4,128,128]{2,1,0:T(8,128)S(1)} %joined.6), channel_id=1, source_target_pairs={{0,8},{4,12},{8,16},{12,20},{16,24},{20,28},{1,9},{5,13},{9,17},{1... | collective-permute-start | bytes 786440 | tf_op jit(solution)/shard_map/ppermute | solution.py:297
  21.3 10.3 %collective-permute-start.11 = (f32[4,128,128]{2,1,0:T(8,128)S(1)}, f32[4,128,128]{2,1,0:T(8,128)S(1)}, u32[]{:S(2)}, u32[]{:S(2)}) collective-permute-start(f32[4,128,128]{2,1,0:T(8,128)S(1)} %joined.7), channel_id=1, source_target_pairs={{0,8},{4,12},{8,16},{12,20},{16,24},{20,28},{1,9},{5,13},{9,17},{1... | collective-permute-start | bytes 786440 | tf_op jit(solution)/shard_map/ppermute | solution.py:297
  31.6 6.6 %copy-start.26 = (bf16[1024]{0:T(1024)(128)(2,1)S(1)}, bf16[1024]{0:T(1024)(128)(2,1)}, u32[]{:S(2)}) copy-start(bf16[1024]{0:T(1024)(128)(2,1)} %param.14) | copy-start | bytes 6148
  35.4 1.2 %collective-permute-start.12 = (f32[24,128]{1,0:T(8,128)S(1)}, f32[24,128]{1,0:T(8,128)S(1)}, u32[]{:S(2)}, u32[]{:S(2)}) collective-permute-start(f32[24,128]{1,0:T(8,128)S(1)} %get-tuple-element.139), channel_id=1, source_target_pairs={{0,1},{1,0},{2,3},{3,2},{4,5},{5,4},{6,7},{7,6},{8,9},{9,8},{10,11... | collective-permute-start | bytes 36872 | tf_op jit(solution)/shard_map/ppermute | solution.py:308
  36.7 3.7 %collective-permute-start.13 = (f32[24,128]{1,0:T(8,128)S(1)}, f32[24,128]{1,0:T(8,128)S(1)}, u32[]{:S(2)}, u32[]{:S(2)}) collective-permute-start(f32[24,128]{1,0:T(8,128)S(1)} %add.18.refs_2_), channel_id=1, source_target_pairs={{0,2},{1,3},{2,0},{3,1},{4,6},{5,7},{6,4},{7,5},{8,10},{9,11},{10,... | collective-permute-start | bytes 36872 | tf_op jit(solution)/shard_map/ppermute | solution.py:308
where the time goes:
time: 44.1 us; the launch traced here: 43.9 us
  Pallas kernels  27.2 us (62%)
  starting transfers between devices  12.4 us (28%)
  waiting for transfers between devices  3.59 us (8%)
    pallas_call x2, Pallas kernels, states_call(): pl.pallas_call(functools.partial(states_kernel, col, first, pairs), in_sp...  9.73 us
    ppermute x2, starting transfers between devices, core(): lax.ppermute(joined_call(doc_starts, dev, states[g][4], other[g]), 'ctx',...  7.69 us
    pallas_call x2, Pallas kernels, across_call(): pl.pallas_call(functools.partial(across_kernel, last), in_specs=[SM, SM]...  7.63 us
    pallas_call x2, Pallas kernels, within_call(): pl.pallas_call(within_kernel, in_specs=[VM] * 4, out_specs=VM, out_shape=...  5.59 us
    ppermute x2, waiting for transfers between devices, core(): lax.ppermute(mine, 'head', [(i, i ^ 1 << bit) for i in range(ways)])  3.29 us
    ppermute x2, starting transfers between devices, core(): other.append(lax.ppermute(states[g][4], 'ctx', beside))  3.09 us
    pallas_call x1, Pallas kernels, norm_call(): pl.pallas_call(functools.partial(norm_kernel, width, groups), in_specs=[V...  3.03 us
    ppermute x2, starting transfers between devices, core(): lax.ppermute(mine, 'head', [(i, i ^ 1 << bit) for i in range(ways)])  1.59 us
  transfers between devices with their start and end apart: 6, of which 3 were waited for; matrix products, arithmetic and copies ran while one was open for 0% of the time, Pallas kernels for 34%

commit v1 on v0

--- a/solution.py
+++ b/solution.py
@@ -11,7 +11,7 @@
 CH = 128
 STEP = 512
 GROUPS = 2
-AHEAD = 4
+AHEAD = 2
 bf16, f32, i32 = jnp.bfloat16, jnp.float32, jnp.int32
 VM = pl.BlockSpec(memory_space=pltpu.VMEM)
 SM = pl.BlockSpec(memory_space=pltpu.SMEM)
@@ -43,7 +43,7 @@
     return count
 
 
-def states_kernel(col, first, pairs, starts_ref, dev_ref, k_hbm, v_hbm, q_hbm, kt_ref, v_ref, q_ref, st_ref, sum_ref, *rest):
+def states_kernel(col, first, pairs, starts_ref, dev_ref, k_hbm, v_hbm, kt_ref, v_ref, st_ref, sum_ref, *rest):
     if first:
         mask_ref, live_ref, hops_ref, kbuf, sem = rest
     else:
@@ -51,16 +51,12 @@
     tokens, feats = v_ref.shape
     heads, chunks, steps, per = feats // HD, tokens // CH, tokens // STEP, STEP // CH
     copies = []
-    for n, (src, dst) in enumerate(((k_hbm, kbuf), (v_hbm, v_ref), (q_hbm, q_ref))):
-        copies.append([])
-        for p in range(steps):
-            rows = pl.ds(p * STEP, STEP)
-            copies[n].append(pltpu.make_async_copy(src.at[rows, pl.ds(col, feats)], dst.at[rows], sem.at[n, p]))
     for p in range(steps):
-        copies[0][p].start()
-        copies[1][p].start()
-    for p in range(steps):
-        copies[2][p].start()
+        rows = pl.ds(p * STEP, STEP)
+        copies.append([pltpu.make_async_copy(src.at[rows, pl.ds(col, feats)], dst.at[rows], sem.at[n, p])
+                       for n, (src, dst) in enumerate(((k_hbm, kbuf), (v_hbm, v_ref)))])
+        for copy in copies[p]:
+            copy.start()
     if first:
         hops, streak, through = jnp.int32(0), jnp.int32(0), jnp.int32(1)
         for p in range(pairs):
@@ -89,8 +85,7 @@
             lower = jnp.broadcast_to(rel[c:c + 1], (CH, CH)).T
             mask_ref[c * CH:(c + 1) * CH, :] = jnp.where(lane >= lower, causal, 0.0)
             live_ref[c * CH:(c + 1) * CH, :] = (lower < 0.0).astype(f32).astype(bf16)
-    for h in range(heads):
-        st_ref[0, h] = jnp.zeros((HD, HD), f32)
+    st_ref[0] = jnp.zeros(st_ref.shape[1:], f32)
 
     def advance(c, h, added):
         for i in (h, h + 1):
@@ -103,8 +98,8 @@
     waiting = []
     for c in range(chunks):
         if c % per == 0:
-            copies[0][c // per].wait()
-            copies[1][c // per].wait()
+            for copy in copies[c // per]:
+                copy.wait()
         rows = slice(c * CH, (c + 1) * CH)
         t = tail[c:c + 1].astype(bf16)
         for h in range(0, heads, 2):
@@ -118,33 +113,28 @@
                 advance(*waiting.pop(0))
     for item in waiting:
         advance(*item)
-    for p in range(steps):
-        copies[2][p].wait()
-
-
-def states_call(col, feats, first, pairs, starts, dev, k, v, q):
+
+def states_call(col, feats, first, pairs, starts, dev, k, v):
     tokens = k.shape[0]
     heads, chunks, steps = feats // HD, tokens // CH, tokens // STEP
-    rows = pltpu.VMEM((tokens, feats), bf16)
-    out = [pltpu.VMEM((feats, tokens), bf16), rows, rows,
+    k, v = (pltpu.with_memory_space_constraint(x, pltpu.HBM) for x in (k, v))
+    out = [pltpu.VMEM((feats, tokens), bf16), pltpu.VMEM((tokens, feats), bf16),
            pltpu.VMEM((chunks, heads, HD, HD), f32), pltpu.VMEM((heads, HD, HD), f32)]
     if first:
         out += [pltpu.VMEM((tokens, CH), f32), pltpu.VMEM((tokens, CH), bf16), jax.ShapeDtypeStruct((2,), i32)]
-    k, v, q = (pltpu.with_memory_space_constraint(x, pltpu.HBM) for x in (k, v, q))
-    return pl.pallas_call(
-        functools.partial(states_kernel, col, first, pairs), in_specs=[SM, SM, HB, HB, HB],
-        out_specs=[VM] * 7 + [SM] if first else [VM] * 5, out_shape=out,
-        scratch_shapes=[pltpu.VMEM((tokens, feats), bf16),
-                        pltpu.SemaphoreType.DMA((3, steps))],
-        compiler_params=params(8), name="states")(starts, dev, k, v, q)
-
-
-def within_kernel(mask_ref, q_ref, kt_ref, v_ref, o_ref):
-    tokens, feats = v_ref.shape
-
-    def finish(rows, both, a, b, hi, lo):
-        vd = diagonal(v_ref[rows, a], v_ref[rows, b])
-        o_ref[rows, both] = mm(hi, vd) + mm(lo, vd)
+    return pl.pallas_call(
+        functools.partial(states_kernel, col, first, pairs), in_specs=[SM, SM, HB, HB],
+        out_specs=[VM] * 6 + [SM] if first else [VM] * 4, out_shape=out,
+        scratch_shapes=[pltpu.VMEM((tokens, feats), bf16), pltpu.SemaphoreType.DMA((2, steps))],
+        compiler_params=params(8), name="states")(starts, dev, k, v)
+
+
+def within_kernel(col, mask_ref, q_ref, kt_ref, v_ref, o_ref):
+    tokens, feats = o_ref.shape
+
+    def finish(rows, h, hi, lo):
+        vd = diagonal(v_ref[rows, h:h + HD], v_ref[rows, h + HD:h + 2 * HD])
+        o_ref[rows, h:h + 2 * HD] = mm(hi, vd) + mm(lo, vd)
 
     waiting = []
     for c in range(tokens // CH):
@@ -152,18 +142,18 @@
         m = mask_ref[rows, :]
         m = jnp.concatenate([m, m], 1)
         for h in range(0, feats, 2 * HD):
-            both, a, b = slice(h, h + 2 * HD), slice(h, h + HD), slice(h + HD, h + 2 * HD)
-            scores = mm(q_ref[rows, both], diagonal(kt_ref[a, rows], kt_ref[b, rows]))
-            waiting.append((rows, both, a, b) + split(scores * m))
+            kd = diagonal(kt_ref[h:h + HD, rows], kt_ref[h + HD:h + 2 * HD, rows])
+            waiting.append((rows, h) + split(mm(q_ref[rows, col + h:col + h + 2 * HD], kd) * m))
             if len(waiting) > AHEAD:
                 finish(*waiting.pop(0))
     for item in waiting:
         finish(*item)
 
 
-def within_call(mask, q, kt, v):
-    return pl.pallas_call(
-        within_kernel, in_specs=[VM] * 4, out_specs=VM, out_shape=pltpu.VMEM(v.shape, f32),
+def within_call(col, feats, mask, q, kt, v):
+    tokens = v.shape[0]
+    return pl.pallas_call(
+        functools.partial(within_kernel, col), in_specs=[VM] * 4, out_specs=VM, out_shape=pltpu.VMEM((tokens, feats), f32),
         compiler_params=params(8), name="within")(mask, q, kt, v)
 
 
@@ -182,20 +172,23 @@
         compiler_params=params(8), name="joined")(starts, dev, own, other)
 
 
-def across_kernel(last, starts_ref, dev_ref, live_ref, q_ref, st_ref, other_ref, planes_ref, att_ref, *rest):
+def across_kernel(last, head, starts_ref, dev_ref, live_ref, q_ref, st_ref, other_ref, att_ref, odd_ref, even_ref, *rest):
     if last:
         sq_in, o_ref, sq_ref, ent = rest
     else:
         o_ref, sq_ref, ent = rest
-    tokens, feats = q_ref.shape
+    tokens, feats = att_ref.shape
     heads = feats // HD
     dev = dev_ref[0]
     odd = dev % 2
     anchor = dev * tokens
     empty = (starts_in(starts_ref, anchor - tokens, anchor) == 0).astype(f32)
     one, zero = jnp.float32(1.0), jnp.float32(0.0)
-    ent[...] = other_ref[...] * jnp.where(odd == 1, one, zero) + planes_ref[...] * jnp.where(
-        dev < 2, zero, jnp.where(odd == 1, empty, one))
+    ent[1] = jnp.zeros(ent.shape[1:], f32)
+    plane = jnp.where(dev < 2, zero, jnp.where(odd == 1, empty, one))
+    second = dev // 2 % 2 == 1
+    ent[0] = (other_ref[...] * jnp.where(odd == 1, one, zero) + odd_ref[...] * jnp.where(second, plane, zero)
+              + even_ref[...] * jnp.where(second, zero, plane))
     first = jnp.int32(tokens)
     for d in range(starts_ref.shape[0]):
         s = starts_ref[d] - anchor
@@ -218,12 +211,12 @@
     for c in range(tokens // CH):
         rows = slice(c * CH, (c + 1) * CH)
         lv = live_ref[rows, :]
-        reach = jnp.where(c * CH <= first, one, zero)
+        gone = (c * CH > first).astype(i32)
         for h in range(0, heads, 2):
             x = []
             for i in (h, h + 1):
-                parts = split(st_ref[c, i] + ent[i] * reach)
-                y = mm(q_ref[rows, i * HD:(i + 1) * HD] * lv, jnp.concatenate(parts, 1))
+                parts = split(st_ref[c, i] + ent[gone, i])
+                y = mm(q_ref[rows, (head + i) * HD:(head + i + 1) * HD] * lv, jnp.concatenate(parts, 1))
                 x.append(y[:, :HD] + y[:, HD:])
             waiting.append((c, h, jnp.concatenate(x, 1)))
             if len(waiting) > AHEAD:
@@ -232,15 +225,15 @@
         finish(*item)
 
 
-def across_call(starts, dev, live, q, st, other, planes, att, sq=None):
+def across_call(head, starts, dev, live, q, st, other, planes, att, sq=None):
     tokens, feats = att.shape
     last = sq is not None
-    args = (starts, dev, live, q, st, other, planes, att) + ((sq,) if last else ())
-    return pl.pallas_call(
-        functools.partial(across_kernel, last), in_specs=[SM, SM] + [VM] * (len(args) - 2), out_specs=[VM, VM],
+    args = (starts, dev, live, q, st, other, att, *planes) + ((sq,) if last else ())
+    return pl.pallas_call(
+        functools.partial(across_kernel, last, head), in_specs=[SM, SM] + [VM] * (len(args) - 2), out_specs=[VM, VM],
         out_shape=[pltpu.VMEM(att.shape, f32), pltpu.VMEM((tokens // CH, CH), f32)],
-        scratch_shapes=[pltpu.VMEM(other.shape, f32)],
-        input_output_aliases={7: 0}, compiler_params=params(8), name="across")(*args)
+        scratch_shapes=[pltpu.VMEM((2,) + other.shape, f32)],
+        input_output_aliases={6: 0}, compiler_params=params(8), name="across")(*args)
 
 
 def norm_kernel(width, groups, *refs):
@@ -274,7 +267,7 @@
         functools.partial(norm_kernel, width, groups), in_specs=[VM] * (groups + 3), out_specs=HB,
         out_shape=pltpu.HBM((tokens, feats * groups), bf16),
         scratch_shapes=[pltpu.VMEM((tokens, feats * groups), bf16), pltpu.SemaphoreType.DMA((tokens // STEP,))],
-        compiler_params=params(10), name="norm")(*atts, mine, theirs, gain)
+        compiler_params=params(8), name="norm")(*atts, mine, theirs, gain)
 
 
 def core(general, dev, query_rows, key_rows, value_rows, out_gain, doc_starts):
@@ -283,26 +276,37 @@
     feats = features // GROUPS
     beside = [(i, i ^ 1) for i in range(slabs)]
     onward = [(i, i + 2) for i in range(slabs - 2)]
+    both = ("ctx", "head")
+
+    def swaps(odd):
+        to = []
+        for me in range(slabs * ways):
+            p = me // (2 * ways)
+            mate = p + 1 if p % 2 == odd else p - 1
+            to.append((me, me + (mate - p) * 2 * ways if 0 <= mate < slabs // 2 else me ^ 1))
+        return to
+
     states, other = [], []
     for g in range(GROUPS):
-        states.append(states_call(g * feats, feats, g == 0, slabs // 2, doc_starts, dev, key_rows, value_rows, query_rows))
-        other.append(lax.ppermute(states[g][4], "ctx", beside))
-    mask, live, hops = states[0][5:]
+        states.append(states_call(g * feats, feats, g == 0, slabs // 2, doc_starts, dev, key_rows, value_rows))
+        other.append(lax.ppermute(states[g][3], "ctx", beside))
+    mask, live, hops = states[0][4:]
+    queries = pltpu.with_memory_space_constraint(query_rows, pltpu.VMEM)
     planes, atts = [], []
     for g in range(GROUPS):
-        kt, v, q = states[g][:3]
-        atts.append(within_call(mask, q, kt, v))
+        atts.append(within_call(g * feats, feats, mask, queries, *states[g][:2]))
         if g == 0:
             other[g], atts[g] = lax.optimization_barrier((other[g], atts[g]))
-        planes.append(lax.ppermute(joined_call(doc_starts, dev, states[g][4], other[g]), "ctx", onward))
+        joined = joined_call(doc_starts, dev, states[g][3], other[g])
+        planes.append([lax.ppermute(joined, both, swaps(odd)) for odd in (0, 1)])
     sq = None
     for g in range(GROUPS):
-        q, st = states[g][2:4]
         far = planes[g]
         if general:
             through = hops[1].astype(f32)
-            far = lax.fori_loop(0, hops[0], lambda _, p: planes[g] + through * lax.ppermute(p, "ctx", onward), far)
-        atts[g], sq = across_call(doc_starts, dev, live, q, st, other[g], far, atts[g], sq)
+            near = jnp.where(dev[0] // 2 % 2 == 1, far[0], far[1]) * jnp.where(dev[0] < 2, 0.0, 1.0)
+            far = [lax.fori_loop(0, hops[0], lambda _, p: near + through * lax.ppermute(p, "ctx", onward), near)] * 2
+        atts[g], sq = across_call(g * feats // HD, doc_starts, dev, live, queries, states[g][2], other[g], far, atts[g], sq)
     mine = sq
     for bit in range(ways.bit_length() - 1):
         theirs = lax.ppermute(mine, "head", [(i, i ^ (1 << bit)) for i in range(ways)])

time: 44.1 us -> 41.8 us (0.948)
  starting transfers between devices: 12.4 us -> 9.54 us
  waiting for transfers between devices: 3.59 us -> 5.09 us
  Pallas kernels: 27.2 us -> 26.2 us
    ppermute x4 -> x6, starting transfers between devices: 10.8 us -> 7.66 us  [the longest x4 4.23 us: core(): planes.append([lax.ppermute(joined, both, swaps(odd)) for odd in (0, 1)])]
    ppermute x4 -> x6, waiting for transfers between devices: 0.3 us -> 2.09 us  [the longest x2 1.54 us: core(): other.append(lax.ppermute(states[g][3], 'ctx', beside))]
    pallas_call x2, Pallas kernels: 9.73 us -> 8.77 us  [states_call(): pl.pallas_call(functools.partial(states_kernel, col, first, pairs), in_sp...]
  transfers between devices with their start and end apart: 6 -> 8, of which waited for: 3 -> 5; matrix products, arithmetic and copies ran while one was open for 0% -> 0% of each run, Pallas kernels for 34% -> 36%
where the time goes in v1:
time: 41.8 us; the launch traced here: 41.6 us
  Pallas kernels  26.2 us (63%)
  starting transfers between devices  9.54 us (23%)
  waiting for transfers between devices  5.09 us (12%)
    pallas_call x2, Pallas kernels, states_call(): pl.pallas_call(functools.partial(states_kernel, col, first, pairs), in_sp...  8.77 us
    pallas_call x2, Pallas kernels, across_call(): pl.pallas_call(functools.partial(across_kernel, last, head), in_specs=[SM...  7.49 us
    pallas_call x2, Pallas kernels, within_call(): pl.pallas_call(functools.partial(within_kernel, col), in_specs=[VM] * 4,...  5.7 us
    ppermute x4, starting transfers between devices, core(): planes.append([lax.ppermute(joined, both, swaps(odd)) for odd in (0, 1)])  4.23 us
    ppermute x2, starting transfers between devices, core(): other.append(lax.ppermute(states[g][3], 'ctx', beside))  3.43 us
    pallas_call x1, Pallas kernels, norm_call(): pl.pallas_call(functools.partial(norm_kernel, width, groups), in_specs=[V...  3.03 us
    ppermute x2, waiting for transfers between devices, core(): lax.ppermute(mine, 'head', [(i, i ^ 1 << bit) for i in range(ways)])  3 us
    ppermute x2, starting transfers between devices, core(): lax.ppermute(mine, 'head', [(i, i ^ 1 << bit) for i in range(ways)])  1.88 us
  transfers between devices with their start and end apart: 8, of which 5 were waited for; matrix products, arithmetic and copies ran while one was open for 0% of the time, Pallas kernels for 36%

profile of v1, /device:TPU:0, one launch (start us, length us, event | category | flops | bytes accessed | tf_op | source)
XLA Modules:
  0.0 41.6 jit_solution(17115949658494324359)
XLA Ops:
  0.0 0.1 pad_add_fusion.dev_ref
  0.1 0.0 copy-start.18
  0.1 4.7 %states.6 = (bf16[512,3072]{1,0:T(8,128)(2,1)S(1)}, bf16[3072,512]{1,0:T(8,128)(2,1)S(1)}, f32[24,4,128,128]{3,2,1,0:T(8,128)S(1)}, f32[4,128,128]{2,1,0:T(8,128...) custom-call(s32[16]{0:T(128)} %starts_ref.11, s32[2]{0:T(128)S(1)} %pad_add_fusion.dev_ref, ...), custom_call_target="tpu_custom_call" | custom-call | tf_op jit(solution)/shard_map/states/pallas_call | solution.py:125
  4.7 0.0 slice-start
  4.8 0.0 slice-start.1
  4.8 3.0 %collective-permute-start.10 = (f32[4,128,128]{2,1,0:T(8,128)S(1)}, f32[4,128,128]{2,1,0:T(8,128)S(1)}, u32[]{:S(2)}, u32[]{:S(2)}) collective-permute-start(f32[4,128,128]{2,1,0:T(8,128)S(1)} %get-tuple-element.123.own_ref), channel_id=1, source_target_pairs={{0,4},{4,0},{8,12},{12,8},{16,20},{20,16},{24,28},{28,24},{1,5},{5... | collective-permute-start | bytes 786440 | tf_op jit(solution)/shard_map/ppermute | solution.py:292
  7.8 0.0 copy-done.18
  7.8 4.1 %states.7 = (bf16[512,3072]{1,0:T(8,128)(2,1)S(1)}, bf16[3072,512]{1,0:T(8,128)(2,1)S(1)}, f32[24,4,128,128]{3,2,1,0:T(8,128)S(1)}, f32[4,128,128]{2,1,0:T(8,128)S(1)}) custom-call(s32[16]{0:T(128)S(1)} %copy-done.18, s32[2]{0:T(128)S(1)} %pad_add_fusion.dev_ref, bf16[3072,1024]{1,0:T(8,128)(2,1)} %k_hbm.3, bf16[3072,1024]{1,0:T(8,128)(2,1)} %v_hbm.3), custom_call_target="tpu_custom_call" | custom-call | tf_op jit(solution)/shard_map/states/pallas_call | solution.py:125
  11.9 0.4 %collective-permute-start.13 = (f32[4,128,128]{2,1,0:T(8,128)S(1)}, f32[4,128,128]{2,1,0:T(8,128)S(1)}, u32[]{:S(2)}, u32[]{:S(2)}) collective-permute-start(f32[4,128,128]{2,1,0:T(8,128)S(1)} %get-tuple-element.131.own_ref), channel_id=1, source_target_pairs={{0,4},{4,0},{8,12},{12,8},{16,20},{20,16},{24,28},{28,24},{1,5},{5... | collective-permute-start | bytes 786440 | tf_op jit(solution)/shard_map/ppermute | solution.py:292
  12.3 0.0 slice-done
  12.3 0.0 slice-done.1
  12.3 2.9 %within.6.att_ref = f32[3072,512]{1,0:T(8,128)S(1)} custom-call(f32[3072,128]{1,0:T(8,128)S(1)} %get-tuple-element.124.mask_ref, bf16[3072,1024]{1,0:T(8,128)(2,1)S(1)} %bitcast.6, bf16[512,3072]{1,0:T(8,128)(2,1)S(1)} %get-tuple-element.125.kt_ref, bf16[3072,512]{1,0:T(8,128)(2,1)S(1)} %get-tuple-element.126.v_ref), custom_call_target="tpu_custom_call" | custom-call | tf_op jit(solution)/shard_map/within/pallas_call | solution.py:155
  15.2 0.0 collective-permute-done.10.other_ref
  15.2 0.6 %joined.6 = f32[4,128,128]{2,1,0:T(8,128)S(1)} custom-call(s32[16]{0:T(128)S(1)} %copy-done.18, s32[2]{0:T(128)S(1)} %pad_add_fusion.dev_ref, f32[4,128,128]{2,1,0:T(8,128)S(1)} %get-tuple-element.123.own_ref, f32[4,128,128]{2,1,0:T(8,128)S(1)} %collective-permute-done.10.other_ref), custom_call_target="tpu_custom_call" | custom-call | tf_op jit(solution)/shard_map/joined/pallas_call | solution.py:170
  15.8 2.4 %collective-permute-start.11 = (f32[4,128,128]{2,1,0:T(8,128)S(1)}, f32[4,128,128]{2,1,0:T(8,128)S(1)}, u32[]{:S(2)}, u32[]{:S(2)}) collective-permute-start(f32[4,128,128]{2,1,0:T(8,128)S(1)} %joined.6), channel_id=1, source_target_pairs={{0,8},{1,9},{2,10},{3,11},{4,12},{5,13},{6,14},{7,15},{8,0},{9,1},... | collective-permute-start | bytes 786440 | tf_op jit(solution)/shard_map/ppermute | solution.py:301
  18.2 0.0 collective-permute-start.12
  18.2 1.5 %collective-permute-done.13.other_ref = f32[4,128,128]{2,1,0:T(8,128)S(1)} collective-permute-done((f32[4,128,128]{2,1,0:T(8,128)S(1)}, f32[4,128,128]{2,1,0:T(8,128)S(1)}, u32[]{:S(2)}, u32[]{:S(2)}) %collective-permute-start.13) | collective-permute-done | bytes 262176 | tf_op jit(solution)/shard_map/ppermute | solution.py:292
  19.7 0.6 %joined.7 = f32[4,128,128]{2,1,0:T(8,128)S(1)} custom-call(s32[16]{0:T(128)S(1)} %copy-done.18, s32[2]{0:T(128)S(1)} %pad_add_fusion.dev_ref, f32[4,128,128]{2,1,0:T(8,128)S(1)} %get-tuple-element.131.own_ref, f32[4,128,128]{2,1,0:T(8,128)S(1)} %collective-permute-done.13.other_ref), custom_call_target="tpu_custom_call" | custom-call | tf_op jit(solution)/shard_map/joined/pallas_call | solution.py:170
  20.3 1.9 %collective-permute-start.14 = (f32[4,128,128]{2,1,0:T(8,128)S(1)}, f32[4,128,128]{2,1,0:T(8,128)S(1)}, u32[]{:S(2)}, u32[]{:S(2)}) collective-permute-start(f32[4,128,128]{2,1,0:T(8,128)S(1)} %joined.7), channel_id=1, source_target_pairs={{0,8},{1,9},{2,10},{3,11},{4,12},{5,13},{6,14},{7,15},{8,0},{9,1},... | collective-permute-start | bytes 786440 | tf_op jit(solution)/shard_map/ppermute | solution.py:301
  22.2 0.0 collective-permute-start.15
  22.2 2.9 %within.7.att_ref = f32[3072,512]{1,0:T(8,128)S(1)} custom-call(f32[3072,128]{1,0:T(8,128)S(1)} %get-tuple-element.124.mask_ref, bf16[3072,1024]{1,0:T(8,128)(2,1)S(1)} %bitcast.6, bf16[512,3072]{1,0:T(8,128)(2,1)S(1)} %get-tuple-element.132.kt_ref, bf16[3072,512]{1,0:T(8,128)(2,1)S(1)} %get-tuple-element.133.v_ref), custom_call_target="tpu_custom_call" | custom-call | tf_op jit(solution)/shard_map/within/pallas_call | solution.py:155
  25.1 0.4 collective-permute-done.11.odd_ref
  25.4 0.0 collective-permute-done.12.even_ref
  25.4 3.8 %across.6 = (f32[3072,512]{1,0:T(8,128)S(1)}, f32[24,128]{1,0:T(8,128)S(1)}) custom-call(s32[16]{0:T(128)S(1)} %copy-done.18, s32[2]{0:T(128)S(1)} %pad_add_fusion.dev_ref, bf16[3072,128]{1,0:T(8,128)(2,1)S(1)} %get-tuple-element.121.live_ref, bf16[3072,1024]{1,0:T(8,128)(2,1)S(1)} %bitcast.6, ...), custom_call_target="tpu_custom_call", output_to_operand_aliasing={{0}: (6, {})} | custom-call | tf_op jit(solution)/shard_map/across/pallas_call | solution.py:232
  29.2 0.2 collective-permute-done.14.odd_ref
  29.4 0.0 collective-permute-done.15.even_ref
  29.4 0.0 copy-start.19
  29.4 3.7 %across.7 = (f32[3072,512]{1,0:T(8,128)S(1)}, f32[24,128]{1,0:T(8,128)S(1)}) custom-call(s32[16]{0:T(128)S(1)} %copy-done.18, s32[2]{0:T(128)S(1)} %pad_add_fusion.dev_ref, bf16[3072,128]{1,0:T(8,128)(2,1)S(1)} %get-tuple-element.121.live_ref, bf16[3072,1024]{1,0:T(8,128)(2,1)S(1)} %bitcast.6, ...), custom_call_target="tpu_custom_call", output_to_operand_aliasing={{0}: (6, {})} | custom-call | tf_op jit(solution)/shard_map/across/pallas_call | solution.py:232
  33.1 0.1 collective-permute-start.16
  33.2 1.2 %collective-permute-done.16 = f32[24,128]{1,0:T(8,128)S(1)} collective-permute-done((f32[24,128]{1,0:T(8,128)S(1)}, f32[24,128]{1,0:T(8,128)S(1)}, u32[]{:S(2)}, u32[]{:S(2)}) %collective-permute-start.16) | collective-permute-done | bytes 12320 | tf_op jit(solution)/shard_map/ppermute | solution.py:312
  34.3 1.8 %collective-permute-start.17 = (f32[24,128]{1,0:T(8,128)S(1)}, f32[24,128]{1,0:T(8,128)S(1)}, u32[]{:S(2)}, u32[]{:S(2)}) collective-permute-start(f32[24,128]{1,0:T(8,128)S(1)} %add.24.refs_2_), channel_id=1, source_target_pairs={{0,2},{1,3},{2,0},{3,1},{4,6},{5,7},{6,4},{7,5},{8,10},{9,11},{10,... | collective-permute-start | bytes 36872 | tf_op jit(solution)/shard_map/ppermute | solution.py:312
  36.2 0.0 copy-done.19
  36.2 1.8 %collective-permute-done.17.refs_3_ = f32[24,128]{1,0:T(8,128)S(1)} collective-permute-done((f32[24,128]{1,0:T(8,128)S(1)}, f32[24,128]{1,0:T(8,128)S(1)}, u32[]{:S(2)}, u32[]{:S(2)}) %collective-permute-start.17) | collective-permute-done | bytes 12320 | tf_op jit(solution)/shard_map/ppermute | solution.py:312
  38.0 3.0 %norm.3 = bf16[3072,1024]{1,0:T(8,128)(2,1)} custom-call(f32[3072,512]{1,0:T(8,128)S(1)} %get-tuple-element.129.refs_0_, f32[3072,512]{1,0:T(8,128)S(1)} %get-tuple-element.135.refs_1_, f32[24,128]{1,0:T(8,128)S(1)} %add.24.refs_2_, f32[24,128]{1,0:T(8,128)S(1)} %collective-permute-done.17.refs_3_, bf16[1,1024]{1,0:T(2,128)(2,1)S(1)} %reshape.11.refs_4_), custom_call_target="tpu_custom_call" | custom-call | tf_op jit(solution)/shard_map/norm/pallas_call | solution.py:266
  41.1 0.3 conditional.1
  (3 shorter events, 0.0 us)
Async XLA Ops:
  0.1 7.7 %copy-start.18 = (s32[16]{0:T(128)S(1)}, s32[16]{0:T(128)}, u32[]{:S(2)}) copy-start(s32[16]{0:T(128)} %starts_ref.11) | copy-start | bytes 196
  4.7 7.6 %slice-start = ((s8[6291456]{0:T(1024)(128)(4,1)}), s8[4194304]{0:T(1024)(128)(4,1)S(1)}, s32[]{:S(2)}) async-start(s8[6291456]{0:T(1024)(128)(4,1)} %bitcast.5), calls=%async_computation | async-start | bytes 8388608
  4.8 7.6 %slice-start.1 = ((s8[6291456]{0:T(1024)(128)(4,1)}), s8[2097152]{0:T(1024)(128)(4,1)S(1)}, s32[]{:S(2)}) async-start(s8[6291456]{0:T(1024)(128)(4,1)} %bitcast.5), calls=%async_computation.1 | async-start | bytes 4194304
  4.8 10.4 %collective-permute-start.10 = (f32[4,128,128]{2,1,0:T(8,128)S(1)}, f32[4,128,128]{2,1,0:T(8,128)S(1)}, u32[]{:S(2)}, u32[]{:S(2)}) collective-permute-start(f32[4,128,128]{2,1,0:T(8,128)S(1)} %get-tuple-element.123.own_ref), channel_id=1, source_target_pairs={{0,4},{4,0},{8,12},{12,8},{16,20},{20,16},{24,28},{28,24},{1,5},{5... | collective-permute-start | bytes 786440 | tf_op jit(solution)/shard_map/ppermute | solution.py:292
  11.9 7.8 %collective-permute-start.13 = (f32[4,128,128]{2,1,0:T(8,128)S(1)}, f32[4,128,128]{2,1,0:T(8,128)S(1)}, u32[]{:S(2)}, u32[]{:S(2)}) collective-permute-start(f32[4,128,128]{2,1,0:T(8,128)S(1)} %get-tuple-element.131.own_ref), channel_id=1, source_target_pairs={{0,4},{4,0},{8,12},{12,8},{16,20},{20,16},{24,28},{28,24},{1,5},{5... | collective-permute-start | bytes 786440 | tf_op jit(solution)/shard_map/ppermute | solution.py:292
  15.8 9.6 %collective-permute-start.11 = (f32[4,128,128]{2,1,0:T(8,128)S(1)}, f32[4,128,128]{2,1,0:T(8,128)S(1)}, u32[]{:S(2)}, u32[]{:S(2)}) collective-permute-start(f32[4,128,128]{2,1,0:T(8,128)S(1)} %joined.6), channel_id=1, source_target_pairs={{0,8},{1,9},{2,10},{3,11},{4,12},{5,13},{6,14},{7,15},{8,0},{9,1},... | collective-permute-start | bytes 786440 | tf_op jit(solution)/shard_map/ppermute | solution.py:301
  18.2 7.2 %collective-permute-start.12 = (f32[4,128,128]{2,1,0:T(8,128)S(1)}, f32[4,128,128]{2,1,0:T(8,128)S(1)}, u32[]{:S(2)}, u32[]{:S(2)}) collective-permute-start(f32[4,128,128]{2,1,0:T(8,128)S(1)} %joined.6), channel_id=1, source_target_pairs={{0,1},{1,0},{2,3},{3,2},{4,5},{5,4},{6,7},{7,6},{8,16},{9,17},{10,... | collective-permute-start | bytes 786440 | tf_op jit(solution)/shard_map/ppermute | solution.py:301
  20.3 9.1 %collective-permute-start.14 = (f32[4,128,128]{2,1,0:T(8,128)S(1)}, f32[4,128,128]{2,1,0:T(8,128)S(1)}, u32[]{:S(2)}, u32[]{:S(2)}) collective-permute-start(f32[4,128,128]{2,1,0:T(8,128)S(1)} %joined.7), channel_id=1, source_target_pairs={{0,8},{1,9},{2,10},{3,11},{4,12},{5,13},{6,14},{7,15},{8,0},{9,1},... | collective-permute-start | bytes 786440 | tf_op jit(solution)/shard_map/ppermute | solution.py:301
  22.2 7.2 %collective-permute-start.15 = (f32[4,128,128]{2,1,0:T(8,128)S(1)}, f32[4,128,128]{2,1,0:T(8,128)S(1)}, u32[]{:S(2)}, u32[]{:S(2)}) collective-permute-start(f32[4,128,128]{2,1,0:T(8,128)S(1)} %joined.7), channel_id=1, source_target_pairs={{0,1},{1,0},{2,3},{3,2},{4,5},{5,4},{6,7},{7,6},{8,16},{9,17},{10,... | collective-permute-start | bytes 786440 | tf_op jit(solution)/shard_map/ppermute | solution.py:301
  29.4 6.7 %copy-start.19 = (bf16[1024]{0:T(1024)(128)(2,1)S(1)}, bf16[1024]{0:T(1024)(128)(2,1)}, u32[]{:S(2)}) copy-start(bf16[1024]{0:T(1024)(128)(2,1)} %param.14) | copy-start | bytes 6148
  33.1 1.2 %collective-permute-start.16 = (f32[24,128]{1,0:T(8,128)S(1)}, f32[24,128]{1,0:T(8,128)S(1)}, u32[]{:S(2)}, u32[]{:S(2)}) collective-permute-start(f32[24,128]{1,0:T(8,128)S(1)} %get-tuple-element.136), channel_id=1, source_target_pairs={{0,1},{1,0},{2,3},{3,2},{4,5},{5,4},{6,7},{7,6},{8,9},{9,8},{10,11... | collective-permute-start | bytes 36872 | tf_op jit(solution)/shard_map/ppermute | solution.py:312
  34.3 3.7 %collective-permute-start.17 = (f32[24,128]{1,0:T(8,128)S(1)}, f32[24,128]{1,0:T(8,128)S(1)}, u32[]{:S(2)}, u32[]{:S(2)}) collective-permute-start(f32[24,128]{1,0:T(8,128)S(1)} %add.24.refs_2_), channel_id=1, source_target_pairs={{0,2},{1,3},{2,0},{3,1},{4,6},{5,7},{6,4},{7,5},{8,10},{9,11},{10,... | collective-permute-start | bytes 36872 | tf_op jit(solution)/shard_map/ppermute | solution.py:312

commit v2 on v1

--- a/solution.py
+++ b/solution.py
@@ -45,7 +45,7 @@
 
 def states_kernel(col, first, pairs, starts_ref, dev_ref, k_hbm, v_hbm, kt_ref, v_ref, st_ref, sum_ref, *rest):
     if first:
-        mask_ref, live_ref, hops_ref, kbuf, sem = rest
+        mask_ref, live_ref, shares_ref, hops_ref, kbuf, sem = rest
     else:
         kbuf, sem = rest
     tokens, feats = v_ref.shape
@@ -65,6 +65,12 @@
             if 0 < p < pairs - 1:
                 streak = jnp.where(bare, streak + 1, 0)
                 hops = jnp.maximum(hops, streak)
+        odd = dev_ref[0] % 2
+        low = (dev_ref[0] - odd + 1) * tokens
+        empty = (starts_in(starts_ref, low, low + tokens) == 0).astype(f32)
+        one = jnp.float32(1.0)
+        mine, theirs = jnp.where(odd == 1, one, empty), jnp.where(odd == 1, empty, one)
+        shares_ref[...] = jnp.where(lax.broadcasted_iota(i32, shares_ref.shape, 0) == 0, mine, theirs)
         hops_ref[0] = hops
         hops_ref[1] = through
     base = lax.broadcasted_iota(i32, (chunks, CH), 0) * CH
@@ -121,10 +127,11 @@
     out = [pltpu.VMEM((feats, tokens), bf16), pltpu.VMEM((tokens, feats), bf16),
            pltpu.VMEM((chunks, heads, HD, HD), f32), pltpu.VMEM((heads, HD, HD), f32)]
     if first:
-        out += [pltpu.VMEM((tokens, CH), f32), pltpu.VMEM((tokens, CH), bf16), jax.ShapeDtypeStruct((2,), i32)]
+        out += [pltpu.VMEM((tokens, CH), f32), pltpu.VMEM((tokens, CH), bf16), pltpu.VMEM((8, CH), f32),
+                jax.ShapeDtypeStruct((2,), i32)]
     return pl.pallas_call(
         functools.partial(states_kernel, col, first, pairs), in_specs=[SM, SM, HB, HB],
-        out_specs=[VM] * 6 + [SM] if first else [VM] * 4, out_shape=out,
+        out_specs=[VM] * 7 + [SM] if first else [VM] * 4, out_shape=out,
         scratch_shapes=[pltpu.VMEM((tokens, feats), bf16), pltpu.SemaphoreType.DMA((2, steps))],
         compiler_params=params(8), name="states")(starts, dev, k, v)
 
@@ -157,19 +164,14 @@
         compiler_params=params(8), name="within")(mask, q, kt, v)
 
 
-def joined_kernel(starts_ref, dev_ref, own_ref, other_ref, o_ref):
-    tokens = dev_ref[1]
-    odd = dev_ref[0] % 2
-    low = (dev_ref[0] - odd + 1) * tokens
-    empty = (starts_in(starts_ref, low, low + tokens) == 0).astype(f32)
-    one = jnp.float32(1.0)
-    o_ref[...] = own_ref[...] * jnp.where(odd == 1, one, empty) + other_ref[...] * jnp.where(odd == 1, empty, one)
-
-
-def joined_call(starts, dev, own, other):
-    return pl.pallas_call(
-        joined_kernel, in_specs=[SM, SM, VM, VM], out_specs=VM, out_shape=pltpu.VMEM(own.shape, f32),
-        compiler_params=params(8), name="joined")(starts, dev, own, other)
+def joined_kernel(shares_ref, own_ref, other_ref, o_ref):
+    o_ref[...] = own_ref[...] * shares_ref[0:1, :] + other_ref[...] * shares_ref[1:2, :]
+
+
+def joined_call(shares, own, other):
+    return pl.pallas_call(
+        joined_kernel, in_specs=[VM] * 3, out_specs=VM, out_shape=pltpu.VMEM(own.shape, f32),
+        compiler_params=params(8), name="joined")(shares, own, other)
 
 
 def across_kernel(last, head, starts_ref, dev_ref, live_ref, q_ref, st_ref, other_ref, att_ref, odd_ref, even_ref, *rest):
@@ -290,14 +292,14 @@
     for g in range(GROUPS):
         states.append(states_call(g * feats, feats, g == 0, slabs // 2, doc_starts, dev, key_rows, value_rows))
         other.append(lax.ppermute(states[g][3], "ctx", beside))
-    mask, live, hops = states[0][4:]
+    mask, live, shares, hops = states[0][4:]
     queries = pltpu.with_memory_space_constraint(query_rows, pltpu.VMEM)
     planes, atts = [], []
     for g in range(GROUPS):
         atts.append(within_call(g * feats, feats, mask, queries, *states[g][:2]))
         if g == 0:
             other[g], atts[g] = lax.optimization_barrier((other[g], atts[g]))
-        joined = joined_call(doc_starts, dev, states[g][3], other[g])
+        joined = joined_call(shares, states[g][3], other[g])
         planes.append([lax.ppermute(joined, both, swaps(odd)) for odd in (0, 1)])
     sq = None
     for g in range(GROUPS):

time: 41.8 us -> 41.2 us (0.986)
  Pallas kernels: 26.2 us -> 25 us
  waiting for transfers between devices: 5.09 us -> 5.66 us
    pallas_call x2, Pallas kernels: 1.23 us -> 0.06 us  [joined_call(): pl.pallas_call(joined_kernel, in_specs=[VM] * 3, out_specs=VM, out_shape=...]
    ppermute x2, waiting for transfers between devices: 1.54 us -> 2.12 us  [core(): other.append(lax.ppermute(states[g][3], 'ctx', beside))]
  transfers between devices with their start and end apart: 8 -> 8, of which waited for: 5 -> 5; matrix products, arithmetic and copies ran while one was open for 0% -> 0% of each run, Pallas kernels for 36% -> 34%
where the time goes in v2:
time: 41.2 us; the launch traced here: 40.9 us
  Pallas kernels  25 us (61%)
  starting transfers between devices  9.56 us (23%)
  waiting for transfers between devices  5.66 us (14%)
    pallas_call x2, Pallas kernels, states_call(): pl.pallas_call(functools.partial(states_kernel, col, first, pairs), in_sp...  8.72 us
    pallas_call x2, Pallas kernels, across_call(): pl.pallas_call(functools.partial(across_kernel, last, head), in_specs=[SM...  7.49 us
    pallas_call x2, Pallas kernels, within_call(): pl.pallas_call(functools.partial(within_kernel, col), in_specs=[VM] * 4,...  5.7 us
    ppermute x4, starting transfers between devices, core(): planes.append([lax.ppermute(joined, both, swaps(odd)) for odd in (0, 1)])  4.25 us
    ppermute x2, starting transfers between devices, core(): other.append(lax.ppermute(states[g][3], 'ctx', beside))  3.42 us
    pallas_call x1, Pallas kernels, norm_call(): pl.pallas_call(functools.partial(norm_kernel, width, groups), in_specs=[V...  3.03 us
    ppermute x2, waiting for transfers between devices, core(): lax.ppermute(mine, 'head', [(i, i ^ 1 << bit) for i in range(ways)])  2.99 us
    ppermute x2, waiting for transfers between devices, core(): other.append(lax.ppermute(states[g][3], 'ctx', beside))  2.12 us
  transfers between devices with their start and end apart: 8, of which 5 were waited for; matrix products, arithmetic and copies ran while one was open for 0% of the time, Pallas kernels for 34%

profile of v2, /device:TPU:0, one launch (start us, length us, event | category | flops | bytes accessed | tf_op | source)
XLA Modules:
  0.0 40.9 jit_solution(10050018613800999615)
XLA Ops:
  0.0 0.1 pad_add_fusion.dev_ref
  0.1 0.0 copy-start.18
  0.1 4.6 %states.6 = (bf16[512,3072]{1,0:T(8,128)(2,1)S(1)}, bf16[3072,512]{1,0:T(8,128)(2,1)S(1)}, f32[24,4,128,128]{3,2,1,0:T(8,128)S(1)}, f32[4,128,128]{2,1,0:T(8,128...) custom-call(s32[16]{0:T(128)} %starts_ref.7, ...), custom_call_target="tpu_custom_call" | custom-call | tf_op jit(solution)/shard_map/states/pallas_call | solution.py:132
  4.7 0.0 slice-start
  4.7 0.0 slice-start.1
  4.7 3.0 %collective-permute-start.10 = (f32[4,128,128]{2,1,0:T(8,128)S(1)}, f32[4,128,128]{2,1,0:T(8,128)S(1)}, u32[]{:S(2)}, u32[]{:S(2)}) collective-permute-start(f32[4,128,128]{2,1,0:T(8,128)S(1)} %get-tuple-element.125.own_ref), channel_id=1, source_target_pairs={{0,4},{4,0},{8,12},{12,8},{16,20},{20,16},{24,28},{28,24},{1,5},{5... | collective-permute-start | bytes 786440 | tf_op jit(solution)/shard_map/ppermute | solution.py:294
  7.7 0.0 copy-done.18
  7.7 4.1 %states.7 = (bf16[512,3072]{1,0:T(8,128)(2,1)S(1)}, bf16[3072,512]{1,0:T(8,128)(2,1)S(1)}, f32[24,4,128,128]{3,2,1,0:T(8,128)S(1)}, f32[4,128,128]{2,1,0:T(8,128)S(1)}) custom-call(s32[16]{0:T(128)S(1)} %copy-done.18, s32[2]{0:T(128)S(1)} %pad_add_fusion.dev_ref, bf16[3072,1024]{1,0:T(8,128)(2,1)} %k_hbm.3, bf16[3072,1024]{1,0:T(8,128)(2,1)} %v_hbm.3), custom_call_target="tpu_custom_call" | custom-call | tf_op jit(solution)/shard_map/states/pallas_call | solution.py:132
  11.8 0.4 %collective-permute-start.13 = (f32[4,128,128]{2,1,0:T(8,128)S(1)}, f32[4,128,128]{2,1,0:T(8,128)S(1)}, u32[]{:S(2)}, u32[]{:S(2)}) collective-permute-start(f32[4,128,128]{2,1,0:T(8,128)S(1)} %get-tuple-element.134.own_ref), channel_id=1, source_target_pairs={{0,4},{4,0},{8,12},{12,8},{16,20},{20,16},{24,28},{28,24},{1,5},{5... | collective-permute-start | bytes 786440 | tf_op jit(solution)/shard_map/ppermute | solution.py:294
  12.3 0.0 slice-done
  12.3 0.0 slice-done.1
  12.3 2.9 %within.6.att_ref = f32[3072,512]{1,0:T(8,128)S(1)} custom-call(f32[3072,128]{1,0:T(8,128)S(1)} %get-tuple-element.126.mask_ref, bf16[3072,1024]{1,0:T(8,128)(2,1)S(1)} %bitcast.6, bf16[512,3072]{1,0:T(8,128)(2,1)S(1)} %get-tuple-element.127.kt_ref, bf16[3072,512]{1,0:T(8,128)(2,1)S(1)} %get-tuple-element.128.v_ref), custom_call_target="tpu_custom_call" | custom-call | tf_op jit(solution)/shard_map/within/pallas_call | solution.py:162
  15.1 0.0 collective-permute-done.10.other_ref
  15.2 2.4 %collective-permute-start.11 = (f32[4,128,128]{2,1,0:T(8,128)S(1)}, f32[4,128,128]{2,1,0:T(8,128)S(1)}, u32[]{:S(2)}, u32[]{:S(2)}) collective-permute-start(f32[4,128,128]{2,1,0:T(8,128)S(1)} %joined.6), channel_id=1, source_target_pairs={{0,8},{1,9},{2,10},{3,11},{4,12},{5,13},{6,14},{7,15},{8,0},{9,1},... | collective-permute-start | bytes 786440 | tf_op jit(solution)/shard_map/ppermute | solution.py:303
  17.6 0.0 collective-permute-start.12
  17.6 2.1 %collective-permute-done.13.other_ref = f32[4,128,128]{2,1,0:T(8,128)S(1)} collective-permute-done((f32[4,128,128]{2,1,0:T(8,128)S(1)}, f32[4,128,128]{2,1,0:T(8,128)S(1)}, u32[]{:S(2)}, u32[]{:S(2)}) %collective-permute-start.13) | collective-permute-done | bytes 262176 | tf_op jit(solution)/shard_map/ppermute | solution.py:294
  19.7 1.9 %collective-permute-start.14 = (f32[4,128,128]{2,1,0:T(8,128)S(1)}, f32[4,128,128]{2,1,0:T(8,128)S(1)}, u32[]{:S(2)}, u32[]{:S(2)}) collective-permute-start(f32[4,128,128]{2,1,0:T(8,128)S(1)} %joined.7), channel_id=1, source_target_pairs={{0,8},{1,9},{2,10},{3,11},{4,12},{5,13},{6,14},{7,15},{8,0},{9,1},... | collective-permute-start | bytes 786440 | tf_op jit(solution)/shard_map/ppermute | solution.py:303
  21.6 0.0 collective-permute-start.15
  21.6 2.8 %within.7.att_ref = f32[3072,512]{1,0:T(8,128)S(1)} custom-call(f32[3072,128]{1,0:T(8,128)S(1)} %get-tuple-element.126.mask_ref, bf16[3072,1024]{1,0:T(8,128)(2,1)S(1)} %bitcast.6, bf16[512,3072]{1,0:T(8,128)(2,1)S(1)} %get-tuple-element.135.kt_ref, bf16[3072,512]{1,0:T(8,128)(2,1)S(1)} %get-tuple-element.136.v_ref), custom_call_target="tpu_custom_call" | custom-call | tf_op jit(solution)/shard_map/within/pallas_call | solution.py:162
  24.4 0.4 collective-permute-done.11.odd_ref
  24.8 0.0 collective-permute-done.12.even_ref
  24.8 3.8 %across.6 = (f32[3072,512]{1,0:T(8,128)S(1)}, f32[24,128]{1,0:T(8,128)S(1)}) custom-call(s32[16]{0:T(128)S(1)} %copy-done.18, s32[2]{0:T(128)S(1)} %pad_add_fusion.dev_ref, bf16[3072,128]{1,0:T(8,128)(2,1)S(1)} %get-tuple-element.123.live_ref, bf16[3072,1024]{1,0:T(8,128)(2,1)S(1)} %bitcast.6, ...), custom_call_target="tpu_custom_call", output_to_operand_aliasing={{0}: (6, {})} | custom-call | tf_op jit(solution)/shard_map/across/pallas_call | solution.py:234
  28.6 0.2 collective-permute-done.14.odd_ref
  28.8 0.0 collective-permute-done.15.even_ref
  28.8 0.0 copy-start.19
  28.8 3.7 %across.7 = (f32[3072,512]{1,0:T(8,128)S(1)}, f32[24,128]{1,0:T(8,128)S(1)}) custom-call(s32[16]{0:T(128)S(1)} %copy-done.18, s32[2]{0:T(128)S(1)} %pad_add_fusion.dev_ref, bf16[3072,128]{1,0:T(8,128)(2,1)S(1)} %get-tuple-element.123.live_ref, bf16[3072,1024]{1,0:T(8,128)(2,1)S(1)} %bitcast.6, ...), custom_call_target="tpu_custom_call", output_to_operand_aliasing={{0}: (6, {})} | custom-call | tf_op jit(solution)/shard_map/across/pallas_call | solution.py:234
  32.5 0.1 collective-permute-start.16
  32.6 1.2 %collective-permute-done.16 = f32[24,128]{1,0:T(8,128)S(1)} collective-permute-done((f32[24,128]{1,0:T(8,128)S(1)}, f32[24,128]{1,0:T(8,128)S(1)}, u32[]{:S(2)}, u32[]{:S(2)}) %collective-permute-start.16) | collective-permute-done | bytes 12320 | tf_op jit(solution)/shard_map/ppermute | solution.py:314
  33.7 1.8 %collective-permute-start.17 = (f32[24,128]{1,0:T(8,128)S(1)}, f32[24,128]{1,0:T(8,128)S(1)}, u32[]{:S(2)}, u32[]{:S(2)}) collective-permute-start(f32[24,128]{1,0:T(8,128)S(1)} %add.24.refs_2_), channel_id=1, source_target_pairs={{0,2},{1,3},{2,0},{3,1},{4,6},{5,7},{6,4},{7,5},{8,10},{9,11},{10,... | collective-permute-start | bytes 36872 | tf_op jit(solution)/shard_map/ppermute | solution.py:314
  35.5 0.0 copy-done.19
  35.6 1.8 %collective-permute-done.17.refs_3_ = f32[24,128]{1,0:T(8,128)S(1)} collective-permute-done((f32[24,128]{1,0:T(8,128)S(1)}, f32[24,128]{1,0:T(8,128)S(1)}, u32[]{:S(2)}, u32[]{:S(2)}) %collective-permute-start.17) | collective-permute-done | bytes 12320 | tf_op jit(solution)/shard_map/ppermute | solution.py:314
  37.4 3.0 %norm.3 = bf16[3072,1024]{1,0:T(8,128)(2,1)} custom-call(f32[3072,512]{1,0:T(8,128)S(1)} %get-tuple-element.132.refs_0_, f32[3072,512]{1,0:T(8,128)S(1)} %get-tuple-element.138.refs_1_, f32[24,128]{1,0:T(8,128)S(1)} %add.24.refs_2_, f32[24,128]{1,0:T(8,128)S(1)} %collective-permute-done.17.refs_3_, bf16[1,1024]{1,0:T(2,128)(2,1)S(1)} %reshape.11.refs_4_), custom_call_target="tpu_custom_call" | custom-call | tf_op jit(solution)/shard_map/norm/pallas_call | solution.py:268
  40.5 0.3 conditional.1
  (5 shorter events, 0.1 us)
Async XLA Ops:
  0.1 7.6 %copy-start.18 = (s32[16]{0:T(128)S(1)}, s32[16]{0:T(128)}, u32[]{:S(2)}) copy-start(s32[16]{0:T(128)} %starts_ref.7) | copy-start | bytes 196
  4.7 7.6 %slice-start = ((s8[6291456]{0:T(1024)(128)(4,1)}), s8[4194304]{0:T(1024)(128)(4,1)S(1)}, s32[]{:S(2)}) async-start(s8[6291456]{0:T(1024)(128)(4,1)} %bitcast.5), calls=%async_computation | async-start | bytes 8388608
  4.7 7.6 %slice-start.1 = ((s8[6291456]{0:T(1024)(128)(4,1)}), s8[2097152]{0:T(1024)(128)(4,1)S(1)}, s32[]{:S(2)}) async-start(s8[6291456]{0:T(1024)(128)(4,1)} %bitcast.5), calls=%async_computation.1 | async-start | bytes 4194304
  4.7 10.4 %collective-permute-start.10 = (f32[4,128,128]{2,1,0:T(8,128)S(1)}, f32[4,128,128]{2,1,0:T(8,128)S(1)}, u32[]{:S(2)}, u32[]{:S(2)}) collective-permute-start(f32[4,128,128]{2,1,0:T(8,128)S(1)} %get-tuple-element.125.own_ref), channel_id=1, source_target_pairs={{0,4},{4,0},{8,12},{12,8},{16,20},{20,16},{24,28},{28,24},{1,5},{5... | collective-permute-start | bytes 786440 | tf_op jit(solution)/shard_map/ppermute | solution.py:294
  11.8 7.8 %collective-permute-start.13 = (f32[4,128,128]{2,1,0:T(8,128)S(1)}, f32[4,128,128]{2,1,0:T(8,128)S(1)}, u32[]{:S(2)}, u32[]{:S(2)}) collective-permute-start(f32[4,128,128]{2,1,0:T(8,128)S(1)} %get-tuple-element.134.own_ref), channel_id=1, source_target_pairs={{0,4},{4,0},{8,12},{12,8},{16,20},{20,16},{24,28},{28,24},{1,5},{5... | collective-permute-start | bytes 786440 | tf_op jit(solution)/shard_map/ppermute | solution.py:294
  15.2 9.6 %collective-permute-start.11 = (f32[4,128,128]{2,1,0:T(8,128)S(1)}, f32[4,128,128]{2,1,0:T(8,128)S(1)}, u32[]{:S(2)}, u32[]{:S(2)}) collective-permute-start(f32[4,128,128]{2,1,0:T(8,128)S(1)} %joined.6), channel_id=1, source_target_pairs={{0,8},{1,9},{2,10},{3,11},{4,12},{5,13},{6,14},{7,15},{8,0},{9,1},... | collective-permute-start | bytes 786440 | tf_op jit(solution)/shard_map/ppermute | solution.py:303
  17.6 7.2 %collective-permute-start.12 = (f32[4,128,128]{2,1,0:T(8,128)S(1)}, f32[4,128,128]{2,1,0:T(8,128)S(1)}, u32[]{:S(2)}, u32[]{:S(2)}) collective-permute-start(f32[4,128,128]{2,1,0:T(8,128)S(1)} %joined.6), channel_id=1, source_target_pairs={{0,1},{1,0},{2,3},{3,2},{4,5},{5,4},{6,7},{7,6},{8,16},{9,17},{10,... | collective-permute-start | bytes 786440 | tf_op jit(solution)/shard_map/ppermute | solution.py:303
  19.7 9.1 %collective-permute-start.14 = (f32[4,128,128]{2,1,0:T(8,128)S(1)}, f32[4,128,128]{2,1,0:T(8,128)S(1)}, u32[]{:S(2)}, u32[]{:S(2)}) collective-permute-start(f32[4,128,128]{2,1,0:T(8,128)S(1)} %joined.7), channel_id=1, source_target_pairs={{0,8},{1,9},{2,10},{3,11},{4,12},{5,13},{6,14},{7,15},{8,0},{9,1},... | collective-permute-start | bytes 786440 | tf_op jit(solution)/shard_map/ppermute | solution.py:303
  21.6 7.2 %collective-permute-start.15 = (f32[4,128,128]{2,1,0:T(8,128)S(1)}, f32[4,128,128]{2,1,0:T(8,128)S(1)}, u32[]{:S(2)}, u32[]{:S(2)}) collective-permute-start(f32[4,128,128]{2,1,0:T(8,128)S(1)} %joined.7), channel_id=1, source_target_pairs={{0,1},{1,0},{2,3},{3,2},{4,5},{5,4},{6,7},{7,6},{8,16},{9,17},{10,... | collective-permute-start | bytes 786440 | tf_op jit(solution)/shard_map/ppermute | solution.py:303
  28.8 6.7 %copy-start.19 = (bf16[1024]{0:T(1024)(128)(2,1)S(1)}, bf16[1024]{0:T(1024)(128)(2,1)}, u32[]{:S(2)}) copy-start(bf16[1024]{0:T(1024)(128)(2,1)} %param.14) | copy-start | bytes 6148
  32.5 1.2 %collective-permute-start.16 = (f32[24,128]{1,0:T(8,128)S(1)}, f32[24,128]{1,0:T(8,128)S(1)}, u32[]{:S(2)}, u32[]{:S(2)}) collective-permute-start(f32[24,128]{1,0:T(8,128)S(1)} %get-tuple-element.139), channel_id=1, source_target_pairs={{0,1},{1,0},{2,3},{3,2},{4,5},{5,4},{6,7},{7,6},{8,9},{9,8},{10,11... | collective-permute-start | bytes 36872 | tf_op jit(solution)/shard_map/ppermute | solution.py:314
  33.7 3.7 %collective-permute-start.17 = (f32[24,128]{1,0:T(8,128)S(1)}, f32[24,128]{1,0:T(8,128)S(1)}, u32[]{:S(2)}, u32[]{:S(2)}) collective-permute-start(f32[24,128]{1,0:T(8,128)S(1)} %add.24.refs_2_), channel_id=1, source_target_pairs={{0,2},{1,3},{2,0},{3,1},{4,6},{5,7},{6,4},{7,5},{8,10},{9,11},{10,... | collective-permute-start | bytes 36872 | tf_op jit(solution)/shard_map/ppermute | solution.py:314
